TPU v7x, 256 devices: a whole 4x4x8 slice. The times are simulated.
256 devices in a mesh: ent: 32 (over y, x, core), rel: 8 (over z).
Axes of the slice: x: 4, y: 4, z: 8, core: 2. Of those that a mesh axis runs over, the one named last changes fastest.
Arguments:
- tile_vals: bfloat16 [32, 8, 64, 128, 128], P('ent', 'rel'), may hold values from -192 to 192
- tile_row: int32 [32, 8, 64], P('ent', 'rel'), may hold values from 0 to 3
- tile_rel: int32 [32, 8, 64], P('ent', 'rel'), may hold values from 0 to 1
- tile_src: int32 [32, 8, 64], P('ent', 'rel'), may hold values from 0 to 31
- needed: int32 [32, 8, 32, 1], P('ent', 'rel'), may hold values from 0 to 3
- factors: bfloat16 [16384, 256], P('ent'), may hold values from -6 to 6
- cores: bfloat16 [16, 256, 256], P('rel'), may hold values from -0.5 to 1.5
- basis: float32 [256, 256], replicated, may hold values from -1 to 1
- spectrum: float32 [256], replicated, may hold values from 100 to 1000
Outputs:
- new_factors: bfloat16 [16384, 256], P('ent')
- new_cores: float32 [16, 256, 256], P('rel')
Inputs may be any that keep to these rules, and one draw needn't show every extreme that they name: tile_src names the owner whose single requested block (slot 0 of `needed`) gives the tile's columns. `needed`: every request slot names a block.
All inputs are finite; a program needn't handle non-finite values.
Results may differ from a plain program's by a relative error of at most 0.0081.
Values may be sent and summed in bfloat16 or wider, within the bound.
A program may use at most 64 MiB of HBM per device.

v0:
```python
import jax
import jax.numpy as jnp
from jax import lax
from jax.sharding import PartitionSpec as P

ridge_shift = 1.0


def shards(tile_vals, tile_row, tile_rel, tile_src, needed, factors, cores, basis, spectrum):
    precise = lax.Precision.HIGHEST
    tile_data = tile_vals[0, 0]
    tile_rows = tile_row[0, 0]
    tile_rels = tile_rel[0, 0]
    sources = tile_src[0, 0]
    asked_rows = needed[0, 0]
    count_ent, slot_count = asked_rows.shape
    tile_edge = tile_data.shape[1]
    rank_width = factors.shape[1]
    rel_local = cores.shape[0]
    row_blocks = factors.shape[0] // tile_edge
    slot_total = count_ent * slot_count
    requests = lax.all_to_all(asked_rows, "ent", split_axis=0, concat_axis=0, tiled=True)

    def neighbour(slab_rows):
        whole_table = lax.all_gather(slab_rows, "ent", axis=0, tiled=True).reshape(
            count_ent, row_blocks, tile_edge, rank_width
        )
        fetched = whole_table[jnp.arange(count_ent)[:, None], asked_rows]
        return fetched.reshape(slot_total, tile_edge, rank_width)[sources]

    def grouped(part_data, key_ids, group_count):
        onehot = (key_ids[:, None] == jnp.arange(group_count, dtype=jnp.int32)[None, :]).astype(
            jnp.bfloat16
        )
        flat_part = part_data.reshape(part_data.shape[0], tile_edge * rank_width)
        return jnp.einsum(
            "tg,tx->gx", onehot, flat_part, preferred_element_type=jnp.float32
        ).astype(jnp.bfloat16)

    gathered_old = neighbour(factors)
    left_part = jnp.einsum(
        "tab,tbr->tar", tile_data, gathered_old, preferred_element_type=jnp.float32
    ).astype(jnp.bfloat16)
    forward = grouped(
        left_part, tile_rels * row_blocks + tile_rows, rel_local * row_blocks
    ).reshape(rel_local, row_blocks, tile_edge, rank_width)
    forward_term = jnp.einsum(
        "kbar,ksr->bas", forward, cores, preferred_element_type=jnp.float32
    ).reshape(-1, rank_width)
    own_blocks = factors.reshape(row_blocks, tile_edge, rank_width)
    right_part = jnp.einsum(
        "tab,tar->tbr", tile_data, own_blocks[tile_rows], preferred_element_type=jnp.float32
    ).astype(jnp.bfloat16)
    backward = grouped(right_part, sources * rel_local + tile_rels, slot_total * rel_local).reshape(
        slot_total, rel_local, tile_edge, rank_width
    )
    backward_term = jnp.einsum(
        "skbr,krq->sbq", backward, cores, preferred_element_type=jnp.float32
    ).reshape(count_ent, slot_count, tile_edge, rank_width)
    returned = lax.all_to_all(backward_term, "ent", split_axis=0, concat_axis=0, tiled=True)
    landing = (
        requests.reshape(1, slot_total) == jnp.arange(row_blocks, dtype=jnp.int32)[:, None]
    ).astype(jnp.float32)
    landed = jnp.dot(
        landing,
        returned.reshape(slot_total, tile_edge * rank_width),
        precision=precise,
        preferred_element_type=jnp.float32,
    ).reshape(-1, rank_width)
    gram_total = lax.psum(
        jnp.einsum("ar,as->rs", factors, factors, preferred_element_type=jnp.float32), "ent"
    )
    core_f32 = cores.astype(jnp.float32)
    system_part = jnp.einsum("kab,bc,kdc->ad", core_f32, gram_total, core_f32, precision=precise)
    system_part = system_part + jnp.einsum(
        "kba,bc,kcd->ad", core_f32, gram_total, core_f32, precision=precise
    )
    numerator, system = lax.psum((forward_term + landed, system_part), "rel")
    system = system + ridge_shift * jnp.eye(rank_width, dtype=jnp.float32)
    factor_low = jnp.linalg.cholesky(system)
    new_factors = jax.scipy.linalg.cho_solve((factor_low, True), numerator.T).T.astype(jnp.bfloat16)
    gathered_new = neighbour(new_factors)
    latest = jnp.einsum(
        "tab,tbr->tar", tile_data, gathered_new, preferred_element_type=jnp.float32
    ).astype(jnp.bfloat16)
    summed = grouped(latest, tile_rels * row_blocks + tile_rows, rel_local * row_blocks).reshape(
        rel_local, row_blocks, tile_edge, rank_width
    )
    core_part = jnp.einsum(
        "bar,kbas->krs",
        new_factors.reshape(row_blocks, tile_edge, rank_width),
        summed,
        preferred_element_type=jnp.float32,
    )
    weights = 1.0 / (spectrum[:, None] * spectrum[None, :] + ridge_shift)
    totals = lax.psum(core_part, "ent")
    rotated = jnp.einsum("ri,krs,sj->kij", basis, totals, basis, precision=precise)
    new_cores = jnp.einsum(
        "ir,krs,js->kij", basis, weights[None] * rotated, basis, precision=precise
    )
    return (new_factors, new_cores)


def solution(mesh):
    in_specs = (
        P("ent", "rel", None, None, None),
        P("ent", "rel", None),
        P("ent", "rel", None),
        P("ent", "rel", None),
        P("ent", "rel", None, None),
        P("ent", None),
        P("rel", None, None),
        P(),
        P(),
    )
    out_specs = (P("ent", None), P("rel", None, None))
    return jax.shard_map(shards, mesh=mesh, in_specs=in_specs, out_specs=out_specs, check_vma=False)
```

profile of v0, /device:TPU:1, one launch (start us, length us, event | category | flops | bytes accessed | tf_op | source)
XLA Modules:
  0.0 606.1 jit_solution(6752421999504624473)
XLA Ops:
  7.2 2.2 fusion.37
  9.5 0.7 all-gather.3.cloned.1.call-update
  10.2 1.3 copy.58
  11.5 8.6 %all-to-all-start = ((s32[32,1,1]{2,1,0:T(1,128)}), s32[32,1,1]{2,1,0:T(1,128)S(1)}, u32[]{:S(2)}, u32[]{:S(2)}) async-start(s32[32,1,1]{2,1,0:T(1,128)} %copy.58), calls=%async_computation | async-start | bytes 32768 | tf_op jit(solution)/shard_map/all_to_all | solution.py:22
  20.1 0.7 fusion.34
  20.8 2.7 gather_fusion.2
  23.5 5.5 convert_bitcast_fusion.1
  29.0 6.8 %copy.96 = bf16[8,8,128,256]{3,1,2,0:T(8,128)(2,1)} copy(bf16[8,8,128,256]{2,3,1,0:T(8,128)(2,1)} %bitcast.176) | data formatting | bytes 8388608
  35.9 3.6 convolution_convert_fusion
  39.5 1.1 copy.97
  40.6 3.2 convolution_bitcast_fusion
  43.8 7.6 %all-to-all-start.1 = ((f32[32,1,128,256]{3,2,1,0:T(8,128)}), f32[32,1,128,256]{3,2,1,0:T(8,128)}, u32[]{:S(2)}, u32[]{:S(2)}) async-start(f32[32,1,128,256]{3,2,1,0:T(8,128)} %convolution_bitcast_fusion), calls=%async_computation.1 | async-start | bytes 8388608 | tf_op jit(solution)/shard_map/all_to_all | solution.py:60
  51.6 0.7 reduce.12
  52.3 100.7 %all-reduce.6.cloned.1.call-done = f32[256,256]{1,0:T(8,128)} async-done(((f32[256,256]{1,0:T(8,128)}), f32[256,256]{1,0:T(8,128)}) %all-reduce.6.cloned.1.call-update) | async-done | bytes 262160 | tf_op jit(solution)/shard_map/psum | solution.py:70
  153.0 1.4 fusion.17
  154.5 0.5 convolution_bitcast_fusion.3
  154.9 1.3 fusion.19
  156.3 1.2 fusion.5
  157.5 4.6 copy.98
  162.1 1.5 fusion.31
  163.6 0.4 reshape.241
  164.0 50.2 %all-gather.3.cloned.1.call-done = bf16[16384,256]{1,0:T(8,128)(2,1)} async-done(((bf16[512,256]{1,0:T(8,128)(2,1)}), bf16[16384,256]{1,0:T(8,128)(2,1)}) %all-gather.3.cloned.1.call-update) | async-done | bytes 8388624 | tf_op jit(solution)/shard_map/all_gather | solution.py:25
  214.1 5.4 gather_fusion
  219.6 4.4 gather_fusion.1
  223.9 5.5 convert_bitcast_fusion.2
  229.4 6.8 %copy.94 = bf16[8,8,128,256]{3,1,2,0:T(8,128)(2,1)} copy(bf16[8,8,128,256]{2,3,1,0:T(8,128)(2,1)} %bitcast.177) | data formatting | bytes 8388608
  236.2 2.9 convolution_convert_fusion.2
  239.3 1.1 fusion.4
  240.5 0.3 all-gather.5.cloned.1.call-start
  240.7 69.6 %all-reduce.10.cloned.1.call-done = (f32[256,512]{0,1:T(8,128)}, f32[256,256]{0,1:T(8,128)}) async-done(((f32[256,512]{0,1:T(8,128)}, f32[256,256]{0,1:T(8,128)}), (f32[256,512]{0,1:T(8,128)}, f32[256,256]{0,1:T(8,128)})) %all-reduce.10.cloned.1.call-update) | async-done | bytes 786448 | tf_op jit(solution)/shard_map/psum | solution.py:78
  310.4 1.0 convert_add_fusion
  311.6 1.0 fusion.16
  312.6 11.7 %cholesky.50 = f32[128,128]{1,0:T(8,128)S(1)} custom-call(f32[128,128]{1,0:T(8,128)S(1)} %cholesky.118), custom_call_target="Cholesky" | custom-call | tf_op jit(solution)/shard_map/jit(cholesky)/cholesky | solution.py:80
  324.3 9.8 %custom-call.18 = f32[1,128,128]{1,2,0:T(8,128)S(1)} custom-call(f32[1,128,128]{2,1,0:T(8,128)S(1)} %get-tuple-element.33), custom_call_target="InvertDiagBlocksLowerTriangular" | custom-call | tf_op jit(solution)/shard_map/jit(cholesky)/cholesky | solution.py:80
  334.4 0.3 convolution_subtract_fusion.2
  334.6 11.7 %cholesky.105 = f32[128,128]{1,0:T(8,128)S(1)} custom-call(f32[128,128]{1,0:T(8,128)S(1)} %convolution_subtract_fusion.2), custom_call_target="Cholesky" | custom-call | tf_op jit(solution)/shard_map/jit(cholesky)/cholesky | solution.py:80
  346.4 0.6 compare_reduce_fusion
  348.4 4.2 while.1
  348.7 0.6 fusion.70
  349.3 1.4 bitcast_dynamic-update-slice_fusion.2
  350.7 0.6 fusion.70
  351.3 1.4 bitcast_dynamic-update-slice_fusion.2
  352.7 19.7 %custom-call.19 = f32[2,128,128]{1,2,0:T(8,128)S(1)} custom-call(f32[2,128,128]{2,1,0:T(8,128)S(1)} %get-tuple-element.9), custom_call_target="InvertDiagBlocksLowerTriangular" | custom-call | tf_op jit(solution)/shard_map/jit(_cho_solve)/triangular_solve | solution.py:81
  372.4 0.4 fusion.6
  372.8 0.6 convolution_subtract_fusion.1
  373.4 0.4 fusion.25
  373.8 0.4 fusion.36
  374.2 0.4 convolution_subtract_fusion
  374.6 0.4 convolution_convert_fusion.3
  375.0 0.7 maximum_bitcast_fusion
  375.8 1.1 copy.71
  376.9 66.5 %all-gather.5.cloned.1.call-done = bf16[16384,256]{0,1:T(8,128)(2,1)} async-done(((bf16[512,256]{0,1:T(8,128)(2,1)}), bf16[16384,256]{0,1:T(8,128)(2,1)}) %all-gather.5.cloned.1.call-update) | async-done | bytes 8388624 | tf_op jit(solution)/shard_map/all_gather | solution.py:25
  443.4 12.0 %copy.92 = bf16[16384,256]{1,0:T(8,128)(2,1)} copy(bf16[16384,256]{0,1:T(8,128)(2,1)} %all-gather.5.cloned.1.call-done) | data formatting | bytes 16777216 | tf_op jit(solution)/shard_map/reshape | solution.py:25
  455.4 5.4 gather_fusion.3
  460.8 4.4 gather_fusion.4
  465.2 5.5 convert_bitcast_fusion
  470.6 6.8 %copy.99 = bf16[8,8,128,256]{3,1,2,0:T(8,128)(2,1)} copy(bf16[8,8,128,256]{2,3,1,0:T(8,128)(2,1)} %bitcast.178) | data formatting | bytes 8388608
  477.4 3.0 convolution_convert_fusion.1
  480.6 1.1 convolution_bitcast_fusion.1
  481.9 112.9 %all-reduce.8.cloned.1.call-done = f32[2,256,256]{1,2,0:T(8,128)} async-done(((f32[2,256,256]{1,2,0:T(8,128)}), f32[2,256,256]{1,2,0:T(8,128)}) %all-reduce.8.cloned.1.call-update) | async-done | bytes 524304 | tf_op jit(solution)/shard_map/psum | solution.py:96
  594.8 1.7 fusion.13
  596.5 0.6 convolution_multiply_fusion
  597.1 0.6 fusion.10
  597.7 1.4 fusion.8
  (55 shorter events, 1.4 us)
Async XLA Ops:
  7.2 16.4 %copy-start = (bf16[1,1,64,128,128]{4,3,2,1,0:T(8,128)(2,1)S(1)}, bf16[1,1,64,128,128]{4,3,2,1,0:T(8,128)(2,1)}, u32[]{:S(2)}) copy-start(bf16[1,1,64,128,128]{4,3,2,1,0:T(8,128)(2,1)} %param.9) | copy-start | bytes 6291460
  7.2 13.6 %copy-start.1 = (bf16[512,256]{1,0:T(8,128)(2,1)S(1)}, bf16[512,256]{1,0:T(8,128)(2,1)}, u32[]{:S(2)}) copy-start(bf16[512,256]{1,0:T(8,128)(2,1)} %param.14) | copy-start | bytes 786436
  7.2 145.9 %all-reduce.6.cloned.1.call-start = ((), (), s32[]{:S(2)}) async-start(), calls=%async_computation.2 | async-start | bytes 524288 | tf_op jit(solution)/shard_map/psum | solution.py:70
  9.4 204.7 %all-gather.3.cloned.1.call-start = ((), (), s32[]{:S(2)}) async-start(), calls=%async_computation.3 | async-start | bytes 8650752 | tf_op jit(solution)/shard_map/all_gather | solution.py:25
  11.5 32.2 %all-to-all-start = ((s32[32,1,1]{2,1,0:T(1,128)}), s32[32,1,1]{2,1,0:T(1,128)S(1)}, u32[]{:S(2)}, u32[]{:S(2)}) async-start(s32[32,1,1]{2,1,0:T(1,128)} %copy.58), calls=%async_computation | async-start | bytes 32768 | tf_op jit(solution)/shard_map/all_to_all | solution.py:22
  29.0 6.8 %copy-start.7 = (s32[1,1,64]{2,1,0:T(1,128)S(1)}, s32[1,1,64]{2,1,0:T(1,128)}, u32[]{:S(2)}) copy-start(s32[1,1,64]{2,1,0:T(1,128)} %param.10) | copy-start | bytes 772
  29.0 6.8 %copy-start.8 = (s32[1,1,64]{2,1,0:T(1,128)S(1)}, s32[1,1,64]{2,1,0:T(1,128)}, u32[]{:S(2)}) copy-start(s32[1,1,64]{2,1,0:T(1,128)} %param.11) | copy-start | bytes 772
  29.0 6.8 %copy-start.10 = (s32[1,1,64]{2,1,0:T(1,128)S(1)}, s32[1,1,64]{2,1,0:T(1,128)}, u32[]{:S(2)}) copy-start(s32[1,1,64]{2,1,0:T(1,128)} %param.12) | copy-start | bytes 772
  39.4 1.1 copy-start.2
  43.8 7.8 %copy-start.9 = (s32[1,1,32,1]{2,3,1,0:T(1,128)S(1)}, s32[1,1,32,1]{2,3,1,0:T(1,128)}, u32[]{:S(2)}) copy-start(s32[1,1,32,1]{2,3,1,0:T(1,128)} %param.13) | copy-start | bytes 388
  43.8 113.7 %all-to-all-start.1 = ((f32[32,1,128,256]{3,2,1,0:T(8,128)}), f32[32,1,128,256]{3,2,1,0:T(8,128)}, u32[]{:S(2)}, u32[]{:S(2)}) async-start(f32[32,1,128,256]{3,2,1,0:T(8,128)} %convolution_bitcast_fusion), calls=%async_computation.1 | async-start | bytes 8388608 | tf_op jit(solution)/shard_map/all_to_all | solution.py:60
  51.3 259.0 %all-reduce.10.cloned.1.call-start = ((), (), s32[]{:S(2)}) async-start(), calls=%async_computation.6 | async-start | bytes 1572864 | tf_op jit(solution)/shard_map/psum | solution.py:78
  240.5 202.9 %all-gather.5.cloned.1.call-start = ((), (), s32[]{:S(2)}) async-start(), calls=%async_computation.4 | async-start | bytes 8650752 | tf_op jit(solution)/shard_map/all_gather | solution.py:25
  310.4 62.0 %copy-start.5 = (f32[256,512]{0,1:T(8,128)S(1)}, f32[256,512]{0,1:T(8,128)}, u32[]{:S(2)}) copy-start(f32[256,512]{0,1:T(8,128)} %get-tuple-element.26) | copy-start | bytes 1572868
  375.7 219.1 %all-reduce.8.cloned.1.call-start = ((), (), s32[]{:S(2)}) async-start(), calls=%async_computation.5 | async-start | bytes 1048576 | tf_op jit(solution)/shard_map/psum | solution.py:96
  376.9 103.7 %copy-start.4 = (bf16[512,256]{1,0:T(8,128)(2,1)}, bf16[512,256]{1,0:T(8,128)(2,1)S(1)}, u32[]{:S(2)}) copy-start(bf16[512,256]{1,0:T(8,128)(2,1)S(1)} %copy.71) | copy-start | bytes 786436
  477.4 4.3 copy-start.6
  477.4 117.3 %copy-start.3 = (f32[256,256]{1,0:T(8,128)S(1)}, f32[256,256]{1,0:T(8,128)}, u32[]{:S(2)}) copy-start(f32[256,256]{1,0:T(8,128)} %param.16) | copy-start | bytes 786436
Sparse Core Ops, SparseCore 0:
  11.8 141.1 all-reduce.5
  155.9 58.1 all-gather.2
  240.6 69.7 all-reduce.9
  375.9 67.4 all-gather.4
  481.9 112.8 all-reduce.7
where the time goes:
time: 613 us; the launch traced here: 606 us
  waiting for transfers between devices  401 us (65%)
  local copies, waits for them, and re-layouts  67.8 us (11%)
  other arithmetic  57.9 us (9%)
  matrix products  46.8 us (8%)
  starting transfers between devices  16.7 us (3%)
  between operations  15.9 us (3%)
    all_gather x2, waiting for transfers between devices, neighbour(): lax.all_gather(slab_rows, 'ent', axis=0, tiled=True)  117 us
    psum x1, waiting for transfers between devices, shards(): totals = lax.psum(core_part, 'ent')  113 us
    psum x1, waiting for transfers between devices, shards(): lax.psum(jnp.einsum('ar,as->rs', factors, factors, preferred_element_type...  101 us
    psum x1, waiting for transfers between devices, shards(): numerator, system = lax.psum((forward_term + landed, system_part), 'rel')  69.6 us
    another operation x6, other arithmetic, shards(): factor_low = jnp.linalg.cholesky(system)  34 us
    unnamed x30, local copies, waits for them, and re-layouts  27.6 us
    another operation x3, other arithmetic, shards(): jax.scipy.linalg.cho_solve((factor_low, True), numerator.T)  19.7 us
  transfers between devices with their start and end apart: 7, of which 5 were waited for; matrix products, arithmetic and copies ran while one was open for 6% of the time, Pallas kernels for 0%

commit v1 on v0

v1 whole, which is shorter than its diff:
```python
import functools
import jax
import jax.numpy as jnp
from jax import lax
from jax.experimental import pallas as pl
from jax.experimental.pallas import tpu as pltpu
from jax.sharding import PartitionSpec as P

ridge_shift = 1.0
N_ENT, N_REL = 32, 8
BLK, R, ROWS, TILES, REL_DEV, SLAB = 128, 256, 4, 64, 2, 512
HALF = SLAB // 2
MESH = pl.DeviceIdType.MESH
F32, BF16 = jnp.float32, jnp.bfloat16
HIGH = lax.Precision.HIGHEST
SPOT = {0: 0, -1: 1, 1: 2, 2: 3}


def dot(a, b, dims=((1,), (0,)), precision=None):
    return lax.dot_general(a, b, (dims, ((), ())), precision=precision, preferred_element_type=F32)


def send(src, dst, send_sem, recv_sem, target):
    return pltpu.make_async_remote_copy(
        src_ref=src, dst_ref=dst, send_sem=send_sem, recv_sem=recv_sem, device_id=target, device_id_type=MESH
    )


def wait_bytes(ref, sem):
    pltpu.make_async_copy(ref, ref, sem).wait()


def greet(me_ent, me_rel):
    barrier = pltpu.get_barrier_semaphore()

    def ent_signal(k, carry):
        pl.semaphore_signal(barrier, inc=1, device_id={"ent": lax.rem(me_ent + k, N_ENT)}, device_id_type=MESH)
        return carry

    def rel_signal(k, carry):
        pl.semaphore_signal(barrier, inc=1, device_id={"rel": lax.rem(me_rel + k, N_REL)}, device_id_type=MESH)
        return carry

    lax.fori_loop(1, N_ENT, ent_signal, 0)
    lax.fori_loop(1, N_REL, rel_signal, 0)
    pl.semaphore_wait(barrier, N_ENT + N_REL - 2)


def spread(axis, count, me, source_at, landing, send_sem, recv_sem):
    def one(k, carry):
        other = lax.rem(me + k, count)
        send(source_at(other), landing.at[me], send_sem, recv_sem, {axis: other}).start()
        return carry

    lax.fori_loop(1, count, one, 0)


def spread_wait(count, landing, source, send_sem, recv_sem):
    wait_bytes(landing.at[pl.ds(0, count - 1)], recv_sem)
    wait_bytes(landing.at[pl.ds(0, count - 1)], send_sem)


def ring_gather(me, own, table, send_sem, recv_sem):
    core = lax.rem(me, 2)
    col = lax.rem(me // 2, 4)
    row = me // 8
    way = 1 - 2 * core
    sibling = me + way

    def at(h, u, v):
        du, dv = (u, v) if h == 0 else (v, u)
        x = lax.rem(col + du * way + 8, 4)
        y = lax.rem(row + dv * way + 8, 4)
        return (y * 4 + x) * 2 + core

    def part(ref, h):
        return ref.at[pl.ds(h * HALF, HALF)]

    def go(h, u, v, target):
        slab = at(h, u, v)
        dst = part(table.at[slab], h)
        src = part(own, h) if (u, v) == (0, 0) else dst
        send(src, dst, send_sem, recv_sem.at[h, slab], {"ent": target}).start()

    def arrive(h, slab):
        dst = part(table.at[slab], h)
        pltpu.make_async_copy(dst, dst, recv_sem.at[h, slab]).wait()

    def first(h):
        go(h, 0, 0, at(h, 1, 0))
        go(h, 0, 0, at(h, -1, 0))
        go(h, 0, 0, at(h, 0, 1))
        go(h, 0, 0, at(h, 0, -1))
        go(h, 0, 0, sibling)

    def along_u(h, u):
        arrive(h, at(h, u, 0))
        if u == -1:
            go(h, u, 0, at(h, 1, 0))
        go(h, u, 0, at(h, 0, 1))
        go(h, u, 0, at(h, 0, -1))
        go(h, u, 0, sibling)

    def along_v(h, u, v):
        arrive(h, at(h, u, v))
        if v == -1:
            go(h, u, v, at(h, 0, 1))
        go(h, u, v, sibling)

    def both(act, *where):
        return lambda: [act(h, *where) for h in (0, 1)]

    steps = [both(first), both(along_u, -1), both(along_u, 1), both(along_v, 0, -1), both(along_v, 0, 1), both(along_u, 2)]
    for u in (-1, 1):
        steps += [both(along_v, u, -1), both(along_v, u, 1)]
    steps += [both(along_v, 0, 2), both(along_v, 2, -1), both(along_v, 2, 1)]
    steps += [both(along_v, u, 2) for u in (-1, 1, 2)]

    def finish():
        def one(k, carry):
            slab = 2 * k + 1 - core
            arrive(0, slab)
            arrive(1, slab)
            return carry

        lax.fori_loop(0, N_ENT // 2, one, 0)
        wait_bytes(table.at[pl.ds(0, N_ENT - 1)], send_sem)

    return steps + [finish]


def sweep(ref):
    size = ref.shape[0]
    rows = lax.broadcasted_iota(jnp.int32, (size, size), 0)
    lanes = lax.broadcasted_iota(jnp.int32, (size, size), 1)
    lane1 = lax.broadcasted_iota(jnp.int32, (1, size), 1)
    row1 = lax.broadcasted_iota(jnp.int32, (size, 1), 0)

    def pivot(k, carry):
        whole = ref[...]
        line = ref[pl.ds(k, 1), :]
        on_lane = lanes == k
        column = jnp.sum(jnp.where(on_lane, whole, 0.0), axis=1, keepdims=True)
        corner = jnp.sum(jnp.where(lane1 == k, line, 0.0), axis=1, keepdims=True)
        line = jnp.where(lane1 == k, -1.0, line) * (1.0 / corner)
        column = jnp.where(row1 == k, -1.0, column)
        ref[...] = jnp.where(on_lane | (rows == k), 0.0, whole) - column * line
        return carry

    return pivot


def sorted_sums(run, count, term, keep_at, start):
    def four(q, carry):
        for i in range(4):
            t = start + q * 4 + i
            run[t + 1] = run[t] * keep_at(t) + term(t)
        return carry

    lax.fori_loop(0, count // 4, four, 0)


def sweep_kernel(
    meta, keeps, needed, tiles, factors, cores, numer_out, inverse_out,
    table, run, terms, landed, req_out, req_in, gram_out, gram_in, gram_all, sys_out, sys_in, sys_all,
    core_wide, core_turn, corner, band, ring_send, ring_recv, pair_send, pair_recv,
):
    ent = lax.axis_index("ent")
    rel = lax.axis_index("rel")
    greet(ent, rel)

    def ask(o, carry):
        req_out[o] = jnp.full((8, 128), needed[o], jnp.int32)
        return carry

    lax.fori_loop(0, N_ENT, ask, 0)
    gram_out[...] = dot(factors[...], factors[...], ((0,), (0,))).reshape(N_ENT, 8, R)
    spread("ent", N_ENT, ent, lambda o: gram_out.at[o], gram_in, pair_send.at[0], pair_recv.at[0])
    gram_in[ent] = gram_out[ent]
    steps = ring_gather(ent, factors, table, ring_send.at[0], ring_recv)
    steps.pop(0)()
    spread("ent", N_ENT, ent, lambda o: req_out.at[o], req_in, pair_send.at[1], pair_recv.at[1])
    req_in[ent] = req_out[ent]
    table[ent] = factors[...]
    for j in range(REL_DEV):
        core_wide[j] = cores[j].astype(F32)
        core_turn[j] = core_wide[j].T
    run[0] = jnp.zeros((BLK, R), F32)

    def backward(t):
        own = factors[pl.ds(meta[4, t] * BLK, BLK), :]
        right = dot(tiles[meta[3, t]], own, ((0,), (0,))).astype(BF16)
        return dot(right, cores[meta[5, t]])

    def backward_part(q):
        sorted_sums(run, 16, backward, lambda t: keeps[1, t], q * 16)

    backward_part(0)
    spread_wait(N_ENT, gram_in, gram_out, pair_send.at[0], pair_recv.at[0])
    gram_all[ent] = jnp.sum(gram_in[...], axis=0)
    spread("ent", N_ENT, ent, lambda o: gram_all.at[ent], gram_all, pair_send.at[2], pair_recv.at[2])
    steps.pop(0)()
    backward_part(1)
    spread_wait(N_ENT, gram_all, gram_all, pair_send.at[2], pair_recv.at[2])
    gram = gram_all[...].reshape(R, R)
    mine = pl.ds(pl.multiple_of(ent * 8, 8), 8)
    part = jnp.zeros((8, R), F32)
    for j in range(REL_DEV):
        left = dot(core_wide[j, mine, :], gram, precision=HIGH)
        part = part + dot(left, core_turn[j], precision=HIGH)
        left = dot(core_turn[j, mine, :], gram, precision=HIGH)
        part = part + dot(left, core_wide[j], precision=HIGH)
    sys_out[...] = part
    spread("rel", N_REL, rel, lambda o: sys_out, sys_in, pair_send.at[3], pair_recv.at[3])
    sys_in[rel] = part
    steps.pop(0)()
    backward_part(2)
    spread_wait(N_REL, sys_in, sys_out, pair_send.at[3], pair_recv.at[3])
    unit = lax.broadcasted_iota(jnp.int32, (8, R), 0) + ent * 8 == lax.broadcasted_iota(jnp.int32, (8, R), 1)
    sys_all[ent] = jnp.sum(sys_in[...], axis=0) + jnp.where(unit, ridge_shift, 0.0)
    spread("ent", N_ENT, ent, lambda o: sys_all.at[ent], sys_all, pair_send.at[4], pair_recv.at[4])
    steps.pop(0)()
    backward_part(3)

    def pack(s, carry):
        terms[s] = (run[meta[7, s]] * keeps[3, s]).astype(BF16)
        return carry

    lax.fori_loop(0, N_ENT, pack, 0)
    spread("ent", N_ENT, ent, lambda o: terms.at[o], landed, pair_send.at[5], pair_recv.at[5])
    landed[ent] = terms[ent]
    spread_wait(N_ENT, sys_all, sys_all, pair_send.at[4], pair_recv.at[4])

    system = sys_all[...].reshape(R, R)
    corner[...] = system[:128, :128]
    band[...] = system[:128, 128:]
    pivot = sweep(corner)
    for i in range(4):
        steps.pop(0)()
        lax.fori_loop(i * 32, i * 32 + 32, pivot, 0)
    first = -corner[...]
    ahead = dot(first, band[...], precision=HIGH)
    low = sys_all[pl.ds(16, 16)].reshape(128, R)[:, 128:]
    corner[...] = low - dot(band[...], ahead, ((0,), (0,)), HIGH)
    for i in range(4):
        steps.pop(0)()
        lax.fori_loop(i * 32, i * 32 + 32, pivot, 0)
    second = -corner[...]
    mixed = dot(ahead, second, precision=HIGH)
    inverse_out[pl.ds(0, 128), pl.ds(0, 128)] = first + dot(mixed, ahead, ((1,), (1,)), HIGH)
    inverse_out[pl.ds(0, 128), pl.ds(128, 128)] = -mixed
    inverse_out[pl.ds(128, 128), pl.ds(0, 128)] = -mixed.T
    inverse_out[pl.ds(128, 128), pl.ds(128, 128)] = second

    for step in steps:
        step()

    def forward(t):
        return dot(tiles[meta[0, t]], table[meta[1, t], pl.ds(meta[2, t] * BLK, BLK), :])

    sorted_sums(run, TILES, forward, lambda t: keeps[0, t], 0)
    spread_wait(N_ENT, req_in, req_out, pair_send.at[1], pair_recv.at[1])
    spread_wait(N_ENT, landed, terms, pair_send.at[5], pair_recv.at[5])
    for b in range(ROWS):
        total = jnp.zeros((BLK, R), F32)
        for j in range(REL_DEV):
            g = j * ROWS + b
            summed = (run[meta[6, g]] * keeps[2, g]).astype(BF16)
            total = total + dot(summed, cores[j], ((1,), (1,)))
        run[b] = total

    def land(c, carry):
        chunk = pl.ds(pl.multiple_of(c * 32, 32), 32)

        def add(o, totals):
            data = landed[o, chunk, :].astype(F32)
            asked = jnp.tile(req_in[o], (4, 2))
            return tuple(totals[b] + jnp.where(asked == b, data, 0.0) for b in range(ROWS))

        totals = lax.fori_loop(0, N_ENT, add, tuple(run[b, chunk, :] for b in range(ROWS)))
        for b in range(ROWS):
            numer_out[pl.ds(pl.multiple_of(b * BLK + c * 32, 32), 32), :] = totals[b].astype(BF16)
        return carry

    lax.fori_loop(0, BLK // 32, land, 0)


def core_kernel(
    meta, keeps, tiles, numer, inverse, basis, spectrum, factors_out, cores_out,
    table, run, numer_in, slab, slice_out, sum_out, sum_in, sum_all, turned, weight,
    ring_send, ring_recv, pair_send, pair_recv,
):
    ent = lax.axis_index("ent")
    rel = lax.axis_index("rel")
    greet(ent, rel)
    piece = SLAB // N_REL

    def rows_of(ref, z):
        return ref.at[pl.ds(pl.multiple_of(z * piece, piece), piece)]

    spread("rel", N_REL, rel, lambda o: rows_of(numer, o), numer_in, pair_send.at[0], pair_recv.at[0])
    numer_in[rel] = numer[pl.ds(pl.multiple_of(rel * piece, piece), piece), :]
    wide = jnp.broadcast_to(spectrum[...], (R, R))
    weight[...] = 1.0 / (wide * wide.T + ridge_shift)
    turned[...] = basis[...].T
    run[0] = jnp.zeros((BLK, R), F32)
    spread_wait(N_REL, numer_in, numer, pair_send.at[0], pair_recv.at[0])
    total = jnp.sum(numer_in[...].astype(F32), axis=0)
    slab[rel] = dot(total, inverse[...], precision=HIGH).astype(BF16)
    spread("rel", N_REL, rel, lambda o: slab.at[rel], slab, pair_send.at[1], pair_recv.at[1])
    spread_wait(N_REL, slab, slab, pair_send.at[1], pair_recv.at[1])
    factors_out[...] = slab[...].reshape(SLAB, R)
    table[ent] = factors_out[...]
    for step in ring_gather(ent, factors_out, table, ring_send.at[0], ring_recv):
        step()

    def latest(t):
        return dot(tiles[meta[0, t]], table[meta[1, t], pl.ds(meta[2, t] * BLK, BLK), :])

    sorted_sums(run, TILES, latest, lambda t: keeps[0, t], 0)
    for j in range(REL_DEV):
        total = jnp.zeros((R, R), F32)
        for b in range(ROWS):
            g = j * ROWS + b
            summed = (run[meta[6, g]] * keeps[2, g]).astype(BF16)
            total = total + dot(factors_out[pl.ds(b * BLK, BLK), :], summed, ((0,), (0,)))
        sum_out[pl.ds(j * 16, 16)] = total.reshape(16, 16, R)
    spread("ent", N_ENT, ent, lambda o: sum_out.at[o], sum_in, pair_send.at[2], pair_recv.at[2])
    sum_in[ent] = sum_out[ent]
    spread_wait(N_ENT, sum_in, sum_out, pair_send.at[2], pair_recv.at[2])
    sum_all[ent] = jnp.sum(sum_in[...], axis=0)
    spread("ent", N_ENT, ent, lambda o: sum_all.at[ent], sum_all, pair_send.at[3], pair_recv.at[3])
    spread_wait(N_ENT, sum_all, sum_all, pair_send.at[3], pair_recv.at[3])
    for j in range(REL_DEV):
        projected = sum_all[pl.ds(j * 16, 16)].reshape(R, R)
        rotated = dot(turned[...], dot(projected, basis[...], precision=HIGH), precision=HIGH)
        rotated = rotated * weight[...]
        cores_out[j] = dot(basis[...], dot(rotated, turned[...], precision=HIGH), precision=HIGH)


def shards(tile_vals, tile_row, tile_rel, tile_src, needed, factors, cores, basis, spectrum):
    rows, rels, sources = tile_row[0, 0], tile_rel[0, 0], tile_src[0, 0]
    asked = needed[0, 0, :, 0]
    order = jnp.arange(TILES, dtype=jnp.int32)
    wanted = jnp.sum(jnp.where(sources[:, None] == jnp.arange(N_ENT)[None, :], asked[None, :], 0), axis=1)

    def arranged(keys, values, groups):
        before = (keys[None, :] < keys[:, None]) | ((keys[None, :] == keys[:, None]) & (order[None, :] < order[:, None]))
        rank = jnp.sum(before.astype(jnp.int32), axis=1)
        here = rank[None, :] == order[:, None]
        keys_sorted, *out = [jnp.sum(jnp.where(here, v[None, :], 0), axis=1) for v in (keys, *values)]
        keep = jnp.concatenate([jnp.zeros((1,), F32), (keys_sorted[1:] == keys_sorted[:-1]).astype(F32)])
        ids = jnp.arange(TILES, dtype=jnp.int32)
        upto = jnp.sum((keys[None, :] <= ids[:, None]).astype(jnp.int32), axis=1)
        some = jnp.any(keys[None, :] == ids[:, None], axis=1).astype(F32)
        return out, keep, upto, some

    fwd, fwd_keep, fwd_last, fwd_some = arranged(rels * ROWS + rows, (order, sources, wanted), 8)
    bwd, bwd_keep, bwd_last, bwd_some = arranged(sources, (order, rows, rels), 32)
    meta = jnp.stack([*fwd, *bwd, fwd_last, bwd_last])
    keeps = jnp.stack([fwd_keep, bwd_keep, fwd_some, bwd_some])
    smem, vmem = pl.BlockSpec(memory_space=pltpu.SMEM), pl.BlockSpec(memory_space=pltpu.VMEM)
    tiles = tile_vals[0, 0]
    ring = [pltpu.SemaphoreType.DMA((1,)), pltpu.SemaphoreType.DMA((2, N_ENT))]
    pairs = [pltpu.SemaphoreType.DMA((6,)), pltpu.SemaphoreType.DMA((6,))]

    numer, inverse = pl.pallas_call(
        sweep_kernel,
        out_shape=[jax.ShapeDtypeStruct((SLAB, R), BF16), jax.ShapeDtypeStruct((R, R), F32)],
        in_specs=[smem] * 3 + [vmem] * 3,
        out_specs=[vmem, vmem],
        scratch_shapes=[
            pltpu.VMEM((N_ENT, SLAB, R), BF16),
            pltpu.VMEM((TILES + 1, BLK, R), F32),
            pltpu.VMEM((N_ENT, BLK, R), BF16),
            pltpu.VMEM((N_ENT, BLK, R), BF16),
            pltpu.VMEM((N_ENT, 8, 128), jnp.int32),
            pltpu.VMEM((N_ENT, 8, 128), jnp.int32),
            pltpu.VMEM((N_ENT, 8, R), F32),
            pltpu.VMEM((N_ENT, 8, R), F32),
            pltpu.VMEM((N_ENT, 8, R), F32),
            pltpu.VMEM((8, R), F32),
            pltpu.VMEM((N_REL, 8, R), F32),
            pltpu.VMEM((N_ENT, 8, R), F32),
            pltpu.VMEM((REL_DEV, R, R), F32),
            pltpu.VMEM((REL_DEV, R, R), F32),
            pltpu.VMEM((128, 128), F32),
            pltpu.VMEM((128, 128), F32),
            *ring,
            *pairs,
        ],
        compiler_params=pltpu.CompilerParams(collective_id=0, has_side_effects=True, vmem_limit_bytes=48 << 20),
        name="numerator_and_inverse",
    )(meta, keeps, asked, tiles, factors, cores)
    return pl.pallas_call(
        core_kernel,
        out_shape=[jax.ShapeDtypeStruct((SLAB, R), BF16), jax.ShapeDtypeStruct((REL_DEV, R, R), F32)],
        in_specs=[smem] * 2 + [vmem] * 5,
        out_specs=[vmem, vmem],
        scratch_shapes=[
            pltpu.VMEM((N_ENT, SLAB, R), BF16),
            pltpu.VMEM((TILES + 1, BLK, R), F32),
            pltpu.VMEM((N_REL, SLAB // N_REL, R), BF16),
            pltpu.VMEM((N_REL, SLAB // N_REL, R), BF16),
            pltpu.VMEM((SLAB // N_REL, R), BF16),
            pltpu.VMEM((N_ENT, 16, R), F32),
            pltpu.VMEM((N_ENT, 16, R), F32),
            pltpu.VMEM((N_ENT, 16, R), F32),
            pltpu.VMEM((R, R), F32),
            pltpu.VMEM((R, R), F32),
            *ring,
            *pairs,
        ],
        compiler_params=pltpu.CompilerParams(collective_id=1, has_side_effects=True, vmem_limit_bytes=48 << 20),
        name="factors_and_cores",
    )(meta, keeps, tiles, numer, inverse, basis, spectrum.reshape(1, R))


def solution(mesh):
    in_specs = (
        P("ent", "rel", None, None, None),
        P("ent", "rel", None),
        P("ent", "rel", None),
        P("ent", "rel", None),
        P("ent", "rel", None, None),
        P("ent", None),
        P("rel", None, None),
        P(),
        P(),
    )
    out_specs = (P("ent", None), P("rel", None, None))
    return jax.shard_map(
        lambda *args: tuple(shards(*args)), mesh=mesh, in_specs=in_specs, out_specs=out_specs, check_vma=False
    )
```

time: 613 us -> 168 us (0.27); the launches traced: 606 us -> 168 us
  waiting for transfers between devices: 401 us -> 0 us
  Pallas kernels: 0 us -> 157 us
  local copies, waits for them, and re-layouts: 67.8 us -> 5.68 us
  other arithmetic: 57.9 us -> 4.65 us
  matrix products: 46.8 us -> 0 us
  starting transfers between devices: 16.7 us -> 0 us
  between operations: 15.9 us -> 0.71 us
    psum x3 -> x0, waiting for transfers between devices: 283 us -> none  [the longest x1 113 us: shards(): totals = lax.psum(core_part, 'ent')]
    pallas_call x0 -> x2, Pallas kernels: none -> 157 us  [the longest x1 86.6 us: shards(): pl.pallas_call(sweep_kernel, out_shape=[jax.ShapeDtypeStruct((SLAB, R), B...]
    all_gather x2 -> x0, waiting for transfers between devices: 117 us -> none  [neighbour(): lax.all_gather(slab_rows, 'ent', axis=0, tiled=True)]
    another operation x9 -> x3, other arithmetic: 53.7 us -> 0.17 us  [shards(): keeps = jnp.stack([fwd_keep, bwd_keep, fwd_some, bwd_some])]
    dot_general x19 -> x0, matrix products: 43.7 us -> none  [the longest x3 9.51 us: grouped(): jnp.einsum('tg,tx->gx', onehot, flat_part, preferred_element_type=jnp.flo...]
    gather x5 -> x0, local copies, waits for them, and re-layouts: 22.4 us -> none  [the longest x2 10.9 us: neighbour(): fetched = whole_table[jnp.arange(count_ent)[:, None], asked_rows]]
    unnamed x30 -> x16, local copies, waits for them, and re-layouts: 27.6 us -> 5.65 us
    all_to_all x2 -> x0, starting transfers between devices: 16.2 us -> none  [the longest x1 8.59 us: shards(): lax.all_to_all(asked_rows, 'ent', split_axis=0, concat_axis=0, tiled=True)]
  transfers between devices with their start and end apart: 7 -> 0, of which waited for: 5 -> 0; matrix products, arithmetic and copies ran while one was open for 6% -> 0% of each run, Pallas kernels for 0% -> 0%
where the time goes in v1:
time: 168 us
  Pallas kernels  157 us (93%)
  local copies, waits for them, and re-layouts  5.68 us (3%)
  other arithmetic  4.65 us (3%)
    pallas_call x1, Pallas kernels, shards(): pl.pallas_call(sweep_kernel, out_shape=[jax.ShapeDtypeStruct((SLAB, R), B...  86.6 us
    pallas_call x1, Pallas kernels, shards(): pl.pallas_call(core_kernel, out_shape=[jax.ShapeDtypeStruct((SLAB, R), BF...  70.3 us
    unnamed x16, local copies, waits for them, and re-layouts  5.65 us

profile of v1, /device:TPU:1, one launch (start us, length us, event | category | flops | bytes accessed | tf_op | source)
XLA Modules:
  0.0 168.0 jit_solution(11839064582767555293)
XLA Ops:
  0.6 0.0 copy-start.5
  0.6 0.7 multiply_add_fusion
  1.3 0.2 convert_reduce_fusion.3
  1.5 0.1 fusion.4
  1.6 0.9 convert_reduce_fusion.2
  2.5 0.8 fusion.5
  3.3 0.8 select_reduce_fusion.8
  4.1 1.0 select_reduce_fusion.1
  5.1 0.1 slice_compare_fusion
  5.2 0.1 fusion.7
  5.2 0.1 fusion.6
  5.3 0.0 copy-start
  5.4 1.6 copy-done
  6.9 0.0 copy-start.2
  6.9 0.9 copy-done.2
  7.9 0.0 copy-start.3
  7.9 0.9 copy-done.3
  8.8 0.0 copy-start.6
  8.8 0.7 copy-done.6
  9.5 0.0 copy-start.1
  9.5 0.0 copy-start.4
  9.5 86.6 %numerator_and_inverse.1 = (bf16[512,256]{1,0:T(8,128)(2,1)S(1)}, f32[256,256]{1,0:T(8,128)S(1)}) custom-call(s32[8,64]{1,0:T(8,128)S(1)} %stack.50.meta, f32[4,64]{1,0:T(4,128)S(1)} %add_convert_fusion.keeps, s32[32]{0:T(128)S(1)} %bitcast.26, bf16[64,128,128]{2,1,0:T(8,128)(2,1)S(1)} %bitcast.22, bf16[512,256]{1,0:T(8,128)(2,1)S(1)} %copy-done.2, ...), custom_call_target="tpu_custom_call" | custom-call | tf_op jit(solution)/shard_map/numerator_and_inverse/pallas_call | solution.py:367
  96.1 0.0 copy-done.5
  96.2 0.0 copy-done.1
  96.2 0.0 copy-done.4
  96.2 70.3 %factors_and_cores.1 = (bf16[512,256]{1,0:T(8,128)(2,1)S(1)}, f32[2,256,256]{2,1,0:T(8,128)S(1)}) custom-call(s32[8,64]{1,0:T(8,128)S(1)} %stack.50.meta, f32[4,64]{1,0:T(4,128)S(1)} %add_convert_fusion.keeps, bf16[64,128,128]{2,1,0:T(8,128)(2,1)S(1)} %bitcast.23, bf16[512,256]{1,0:T(8,128)(2,1)S(1)} %get-tuple-element.4.numer, ...), custom_call_target="tpu_custom_call" | custom-call | tf_op jit(solution)/shard_map/factors_and_cores/pallas_call | solution.py:395
  166.5 0.7 copy.13
  167.2 0.8 copy.14
  (2 shorter events, 0.0 us)
Async XLA Ops:
  0.6 95.5 %copy-start.5 = (f32[256]{0:T(256)S(1)}, f32[256]{0:T(256)}, u32[]{:S(2)}) copy-start(f32[256]{0:T(256)} %param.17) | copy-start | bytes 3076
  5.3 1.6 copy-start
  6.9 0.9 copy-start.2
  7.9 0.9 copy-start.3
  8.8 0.7 copy-start.6
  9.5 86.7 %copy-start.1 = (bf16[1,1,64,128,128]{4,3,2,1,0:T(8,128)(2,1)S(1)}, bf16[1,1,64,128,128]{4,3,2,1,0:T(8,128)(2,1)}, u32[]{:S(2)}) copy-start(bf16[1,1,64,128,128]{4,3,2,1,0:T(8,128)(2,1)} %param.9) | copy-start | bytes 6291460
  9.5 86.7 %copy-start.4 = (f32[256,256]{1,0:T(8,128)S(1)}, f32[256,256]{1,0:T(8,128)}, u32[]{:S(2)}) copy-start(f32[256,256]{1,0:T(8,128)} %basis.1) | copy-start | bytes 786436

commit v2 on v1

v2 whole, which is shorter than its diff:
```python
import functools
import jax
import jax.numpy as jnp
from jax import lax
from jax.experimental import pallas as pl
from jax.experimental.pallas import tpu as pltpu
from jax.sharding import PartitionSpec as P

ridge_shift = 1.0
N_ENT, N_REL = 32, 8
BLK, R, ROWS, TILES, REL_DEV, SLAB = 128, 256, 4, 64, 2, 512
PIECE = SLAB // N_REL
MESH = pl.DeviceIdType.MESH
F32, BF16 = jnp.float32, jnp.bfloat16
HIGH = lax.Precision.HIGHEST
SPOT = {0: 0, -1: 1, 1: 2, 2: 3}


def dot(a, b, dims=((1,), (0,)), precision=None):
    return lax.dot_general(a, b, (dims, ((), ())), precision=precision, preferred_element_type=F32)


def send(src, dst, send_sem, recv_sem, target):
    return pltpu.make_async_remote_copy(
        src_ref=src, dst_ref=dst, send_sem=send_sem, recv_sem=recv_sem, device_id=target, device_id_type=MESH
    )


def wait_bytes(ref, sem):
    pltpu.make_async_copy(ref, ref, sem).wait()


def greet(me_ent, me_rel):
    barrier = pltpu.get_barrier_semaphore()

    def ent_signal(k, carry):
        pl.semaphore_signal(barrier, inc=1, device_id={"ent": lax.rem(me_ent + k, N_ENT)}, device_id_type=MESH)
        return carry

    def rel_signal(k, carry):
        pl.semaphore_signal(barrier, inc=1, device_id={"rel": lax.rem(me_rel + k, N_REL)}, device_id_type=MESH)
        return carry

    lax.fori_loop(1, N_ENT, ent_signal, 0)
    lax.fori_loop(1, N_REL, rel_signal, 0)
    return lambda: pl.semaphore_wait(barrier, N_ENT + N_REL - 2)


def pieces(wide, count):
    out = []
    for _ in range(count):
        out.append(wide.astype(BF16))
        wide = wide - out[-1].astype(F32)
    return out


def dot_pieces(left, right, dims=((1,), (0,))):
    longest = max(len(left), len(right))
    terms = [(i + k, dot(a, b, dims)) for i, a in enumerate(left) for k, b in enumerate(right) if i + k < longest]
    return sum(t for _, t in sorted(terms, key=lambda p: -p[0]))


def spread(axis, count, me, source_at, landing, send_sem, recv_sem):
    def one(k, carry):
        other = lax.rem(me + k, count)
        send(source_at(other), landing.at[me], send_sem, recv_sem, {axis: other}).start()
        return carry

    lax.fori_loop(1, count, one, 0)


def spread_wait(count, landing, source, send_sem, recv_sem):
    wait_bytes(landing.at[pl.ds(0, count - 1)], recv_sem)
    wait_bytes(landing.at[pl.ds(0, count - 1)], send_sem)


def ring_gather(me, own, table, send_sem, recv_sem):
    core = lax.rem(me, 2)
    col = lax.rem(me // 2, 4)
    row = me // 8
    way = 1 - 2 * core
    sibling = me + way

    def at(h, u, v):
        du, dv = (u, v) if h == 0 else (v, u)
        x = lax.rem(col + du * way + 8, 4)
        y = lax.rem(row + dv * way + 8, 4)
        return (y * 4 + x) * 2 + core

    def part(ref, h):
        return ref.at[pl.ds(h * N_REL // 2, N_REL // 2)]

    def go(h, u, v, target):
        slab = at(h, u, v)
        dst = part(table.at[slab], h)
        src = part(own, h) if (u, v) == (0, 0) else dst
        send(src, dst, send_sem, recv_sem.at[h, slab], {"ent": target}).start()

    def arrive(h, slab):
        dst = part(table.at[slab], h)
        pltpu.make_async_copy(dst, dst, recv_sem.at[h, slab]).wait()

    def first(h):
        go(h, 0, 0, at(h, 1, 0))
        go(h, 0, 0, at(h, -1, 0))
        go(h, 0, 0, at(h, 0, 1))
        go(h, 0, 0, at(h, 0, -1))
        go(h, 0, 0, sibling)

    def along_u(h, u):
        arrive(h, at(h, u, 0))
        if u == -1:
            go(h, u, 0, at(h, 1, 0))
        go(h, u, 0, at(h, 0, 1))
        go(h, u, 0, at(h, 0, -1))
        go(h, u, 0, sibling)

    def along_v(h, u, v):
        arrive(h, at(h, u, v))
        if v == -1:
            go(h, u, v, at(h, 0, 1))
        go(h, u, v, sibling)

    def both(act, *where):
        return lambda: [act(h, *where) for h in (0, 1)]

    steps = [both(first), both(along_u, -1), both(along_u, 1), both(along_v, 0, -1), both(along_v, 0, 1), both(along_u, 2)]
    for u in (-1, 1):
        steps += [both(along_v, u, -1), both(along_v, u, 1)]
    steps += [both(along_v, 0, 2), both(along_v, 2, -1), both(along_v, 2, 1)]
    steps += [both(along_v, u, 2) for u in (-1, 1, 2)]

    def finish():
        def one(k, carry):
            slab = 2 * k + 1 - core
            arrive(0, slab)
            arrive(1, slab)
            return carry

        lax.fori_loop(0, N_ENT // 2, one, 0)
        wait_bytes(table.at[pl.ds(0, N_ENT - 1)], send_sem)

    return steps + [finish]


def sweep(ref):
    size = ref.shape[0]
    rows = lax.broadcasted_iota(jnp.int32, (size, size), 0)
    lanes = lax.broadcasted_iota(jnp.int32, (size, size), 1)
    lane1 = lax.broadcasted_iota(jnp.int32, (1, size), 1)
    row1 = lax.broadcasted_iota(jnp.int32, (size, 1), 0)

    def pivot(k, carry):
        whole = ref[...]
        line = ref[pl.ds(k, 1), :]
        on_lane = lanes == k
        column = jnp.sum(jnp.where(on_lane, whole, 0.0), axis=1, keepdims=True)
        corner = jnp.sum(jnp.where(lane1 == k, line, 0.0), axis=1, keepdims=True)
        line = jnp.where(lane1 == k, -1.0, line) * (1.0 / corner)
        column = jnp.where(row1 == k, -1.0, column)
        ref[...] = jnp.where(on_lane | (rows == k), 0.0, whole) - column * line
        return carry

    return pivot


def sorted_sums(run, count, term, keep_at, start):
    def four(q, carry):
        for i in range(4):
            t = start + q * 4 + i
            run[t + 1] = run[t] * keep_at(t) + term(t)
        return carry

    lax.fori_loop(0, count // 4, four, 0)


def arranged(raw, key):
    shape = (128, 128)
    lane = lax.broadcasted_iota(jnp.int32, shape, 1)
    keys = jnp.broadcast_to(raw[key : key + 1, :], shape)
    turned = keys.T
    earlier = (keys == turned) & (lane < lax.broadcasted_iota(jnp.int32, shape, 0))
    rank = jnp.sum(jnp.where((keys < turned) | earlier, 1, 0), axis=1, keepdims=True)
    repeats = jnp.sum(jnp.where(earlier, 1, 0), axis=1, keepdims=True)
    here = rank == lane

    def put(values):
        return jnp.sum(jnp.where(here, values, 0), axis=0, keepdims=True)

    keep = put(jnp.where(repeats > 0, 1, 0))
    upto = jnp.sum(jnp.where(turned <= lane, 1, 0), axis=0, keepdims=True)
    some = jnp.minimum(jnp.sum(jnp.where(turned == lane, 1, 0), axis=0, keepdims=True), 1)
    return put, keep, upto, some


def sweep_kernel(
    rows_in, rels_in, sources_in, needed_in, needed, tiles_hbm, factors_hbm, cores_hbm, basis_hbm, spectrum,
    factors_out, cores_out,
    tiles, factors, cores, basis, raw, meta_wide, keeps_wide, meta, keeps,
    table, fresh, run, ahead_terms, terms, landed, req_out, req_in, sys_out, sys_in, sys_row, sys_rows, sys_all,
    corner, band, inverse, numer_out, numer_in, weight, sum_out, sum_in, sum_all,
    ring_send, ring_recv, pair_send, pair_recv, local,
):
    ent = lax.axis_index("ent")
    rel = lax.axis_index("rel")
    moves = [
        pltpu.make_async_copy(a, b, local.at[i])
        for i, (a, b) in enumerate(
            ((factors_hbm, factors), (cores_hbm, cores), (tiles_hbm, tiles), (basis_hbm, basis))
        )
    ]
    for move in moves:
        move.start()
    all_here = greet(ent, rel)

    moves[0].wait()
    moves[1].wait()
    slab_rows = factors[...].reshape(SLAB, R)
    gram = pieces(dot(slab_rows, slab_rows, ((0,), (0,))), 3)
    share = jnp.zeros((R, R), F32)
    for j in range(REL_DEV):
        left = pieces(dot_pieces([cores[j]], gram), 3)
        share = share + dot_pieces(left, [cores[j]], ((1,), (1,)))
        right = pieces(dot_pieces(gram, [cores[j]]), 3)
        share = share + dot_pieces([cores[j]], right, ((0,), (0,)))
    sys_out[...] = share.reshape(N_ENT, 8, R)
    all_here()
    spread("ent", N_ENT, ent, lambda o: sys_out.at[o], sys_in, pair_send.at[0], pair_recv.at[0])
    sys_in[ent] = sys_out[ent]
    steps = ring_gather(ent, factors, table, ring_send.at[0], ring_recv.at[0])
    steps.pop(0)()

    raw[...] = jnp.full((8, 128), 1000, jnp.int32)
    raw[0:1, 0:TILES] = rels_in[...] * ROWS + rows_in[...]
    raw[1:2, 0:TILES] = sources_in[...]
    raw[2:3, 0:TILES] = rows_in[...]
    raw[3:4, 0:TILES] = rels_in[...]
    raw[4:5, 0:N_ENT] = needed_in[...]
    lane = lax.broadcasted_iota(jnp.int32, (128, 128), 1)
    line = lax.broadcasted_iota(jnp.int32, (128, 128), 0)

    def turn(i):
        return jnp.broadcast_to(raw[i : i + 1, :], (128, 128)).T

    wanted = jnp.sum(jnp.where(lane == turn(1), jnp.broadcast_to(raw[4:5, :], (128, 128)), 0), axis=1, keepdims=True)
    put, keep, upto, some = arranged(raw, 0)
    meta_wide[0:1, :] = put(line)
    meta_wide[1:2, :] = put(turn(1))
    meta_wide[2:3, :] = put(wanted)
    meta_wide[6:7, :] = upto
    keeps_wide[0:1, :] = keep.astype(F32)
    keeps_wide[2:3, :] = some.astype(F32)
    put, keep, upto, some = arranged(raw, 1)
    meta_wide[3:4, :] = put(line)
    meta_wide[4:5, :] = put(turn(2))
    meta_wide[5:6, :] = put(turn(3))
    meta_wide[7:8, :] = upto
    keeps_wide[1:2, :] = keep.astype(F32)
    keeps_wide[3:4, :] = some.astype(F32)
    keeps_wide[4:8, :] = jnp.zeros((4, 128), F32)
    orders = [
        pltpu.make_async_copy(meta_wide, meta, local.at[4]),
        pltpu.make_async_copy(keeps_wide, keeps, local.at[5]),
    ]
    for order in orders:
        order.start()

    def ask(o, carry):
        req_out[o] = jnp.full((8, 128), needed[0, o], jnp.int32)
        return carry

    lax.fori_loop(0, N_ENT, ask, 0)
    req_in[ent] = req_out[ent]
    spread("ent", N_ENT, ent, lambda o: req_out.at[o], req_in, pair_send.at[1], pair_recv.at[1])
    table[ent] = factors[...]
    run[0] = jnp.zeros((BLK, R), F32)
    for order in orders:
        order.wait()
    moves[2].wait()

    def backward(t):
        own = factors[pl.ds(meta[4, t] * 2, 2)].reshape(BLK, R)
        right = dot(tiles[meta[3, t]], own, ((0,), (0,))).astype(BF16)
        return dot(right, cores[meta[5, t]])

    def backward_part(q):
        sorted_sums(run, 16, backward, lambda t: keeps[1, t], q * 16)

    backward_part(0)
    spread_wait(N_ENT, sys_in, sys_out, pair_send.at[0], pair_recv.at[0])
    sys_row[...] = jnp.sum(sys_in[...], axis=0)
    spread("rel", N_REL, rel, lambda o: sys_row, sys_rows, pair_send.at[3], pair_recv.at[3])
    sys_rows[rel] = sys_row[...]
    steps.pop(0)()
    backward_part(1)
    steps.pop(0)()
    backward_part(2)
    spread_wait(N_REL, sys_rows, sys_row, pair_send.at[3], pair_recv.at[3])
    unit = lax.broadcasted_iota(jnp.int32, (8, R), 0) + ent * 8 == lax.broadcasted_iota(jnp.int32, (8, R), 1)
    sys_all[ent] = jnp.sum(sys_rows[...], axis=0) + jnp.where(unit, ridge_shift, 0.0)
    spread("ent", N_ENT, ent, lambda o: sys_all.at[ent], sys_all, pair_send.at[4], pair_recv.at[4])
    steps.pop(0)()
    backward_part(3)
    steps.pop(0)()

    def pack(o):
        return (run[meta[7, o]] * keeps[3, o]).astype(BF16)

    def give(k, carry):
        o = lax.rem(ent + k, N_ENT)
        terms[o] = pack(o)
        send(terms.at[o], landed.at[ent], pair_send.at[5], pair_recv.at[5], {"ent": o}).start()
        return carry

    lax.fori_loop(1, N_ENT, give, 0)
    landed[ent] = pack(ent)
    steps.pop(0)()
    spread_wait(N_ENT, sys_all, sys_all, pair_send.at[4], pair_recv.at[4])

    system = sys_all[...].reshape(R, R)
    corner[...] = system[:128, :128]
    band[...] = system[:128, 128:]
    pivot = sweep(corner)

    def pivots():
        for i in range(8):
            if len(steps) > 1:
                steps.pop(0)()
            lax.fori_loop(i * 16, i * 16 + 16, pivot, 0)

    pivots()
    first = -corner[...]
    ahead = dot(first, band[...], precision=HIGH)
    low = sys_all[pl.ds(16, 16)].reshape(128, R)[:, 128:]
    corner[...] = low - dot(band[...], ahead, ((0,), (0,)), HIGH)
    inverse[pl.ds(0, 128), pl.ds(0, 128)] = first
    band[...] = ahead
    pivots()
    ahead = band[...]
    second = -corner[...]
    mixed = dot(ahead, second, precision=HIGH)
    inverse[pl.ds(0, 128), pl.ds(0, 128)] += dot(mixed, ahead, ((1,), (1,)), HIGH)
    inverse[pl.ds(0, 128), pl.ds(128, 128)] = -mixed
    inverse[pl.ds(128, 128), pl.ds(0, 128)] = -mixed.T
    inverse[pl.ds(128, 128), pl.ds(128, 128)] = second

    for step in steps:
        step()

    def forward(t):
        return dot(tiles[meta[0, t]], table[meta[1, t], pl.ds(meta[2, t] * 2, 2)].reshape(BLK, R))

    sorted_sums(run, TILES, forward, lambda t: keeps[0, t], 0)
    for b in range(ROWS):
        total = jnp.zeros((BLK, R), F32)
        for j in range(REL_DEV):
            g = j * ROWS + b
            summed = (run[meta[6, g]] * keeps[2, g]).astype(BF16)
            total = total + dot(summed, cores[j], ((1,), (1,)))
        ahead_terms[pl.ds(b * 2, 2)] = total.reshape(2, PIECE, R)
    moves[3].wait()
    wide = jnp.broadcast_to(spectrum[...], (R, R))
    weight[...] = 1.0 / (wide * wide.T + ridge_shift)
    spread_wait(N_ENT, req_in, req_out, pair_send.at[1], pair_recv.at[1])
    spread_wait(N_ENT, landed, terms, pair_send.at[5], pair_recv.at[5])

    def landing(q):
        block = q // 2
        chunk = pl.ds(pl.multiple_of(lax.rem(q, 2) * PIECE, PIECE), PIECE)

        def add(o, total):
            return total + jnp.where(jnp.tile(req_in[o], (8, 2)) == block, landed[o, chunk, :].astype(F32), 0.0)

        return lax.fori_loop(0, N_ENT, add, ahead_terms[q])

    def hand_over(k, carry):
        z = lax.rem(rel + k, N_REL)
        numer_out[z] = landing(z).astype(BF16)
        send(numer_out.at[z], numer_in.at[rel], pair_send.at[2], pair_recv.at[2], {"rel": z}).start()
        return carry

    lax.fori_loop(1, N_REL, hand_over, 0)
    numer_in[rel] = jnp.zeros((PIECE, R), BF16)
    mine = landing(rel)
    spread_wait(N_REL, numer_in, numer_out, pair_send.at[2], pair_recv.at[2])
    total = mine + jnp.sum(numer_in[...].astype(F32), axis=0)
    fresh[ent, rel] = dot(total, inverse[...], precision=HIGH).astype(BF16)
    spread("rel", N_REL, rel, lambda o: fresh.at[ent, rel], fresh.at[ent], pair_send.at[6], pair_recv.at[6])
    basis_wide = pieces(basis[...], 2)
    turned = pieces(basis[...].T, 2)
    spread_wait(N_REL, fresh.at[ent], fresh.at[ent], pair_send.at[6], pair_recv.at[6])
    steps = ring_gather(ent, fresh.at[ent], fresh, ring_send.at[1], ring_recv.at[1])
    steps.pop(0)()
    factors_out[...] = fresh[ent].reshape(SLAB, R)
    for step in steps:
        step()

    def latest(t):
        return dot(tiles[meta[0, t]], fresh[meta[1, t], pl.ds(meta[2, t] * 2, 2)].reshape(BLK, R))

    sorted_sums(run, TILES, latest, lambda t: keeps[0, t], 0)
    for j in range(REL_DEV):
        total = jnp.zeros((R, R), F32)
        for b in range(ROWS):
            g = j * ROWS + b
            summed = (run[meta[6, g]] * keeps[2, g]).astype(BF16)
            total = total + dot(fresh[ent, pl.ds(b * 2, 2)].reshape(BLK, R), summed, ((0,), (0,)))
        sum_out[pl.ds(j * 16, 16)] = total.astype(BF16).reshape(16, 16, R)
    spread("ent", N_ENT, ent, lambda o: sum_out.at[o], sum_in, pair_send.at[7], pair_recv.at[7])
    sum_in[ent] = sum_out[ent]
    spread_wait(N_ENT, sum_in, sum_out, pair_send.at[7], pair_recv.at[7])
    sum_all[ent] = jnp.sum(sum_in[...].astype(F32), axis=0).astype(BF16)
    spread("ent", N_ENT, ent, lambda o: sum_all.at[ent], sum_all, pair_send.at[8], pair_recv.at[8])
    spread_wait(N_ENT, sum_all, sum_all, pair_send.at[8], pair_recv.at[8])
    for j in range(REL_DEV):
        projected = sum_all[pl.ds(j * 16, 16)].reshape(R, R)
        half = pieces(dot_pieces([projected], basis_wide), 2)
        rotated = pieces(dot_pieces(turned, half) * weight[...], 2)
        half = pieces(dot_pieces(rotated, turned), 2)
        cores_out[j] = dot_pieces(basis_wide, half)


def shards(tile_vals, tile_row, tile_rel, tile_src, needed, factors, cores, basis, spectrum):
    smem, vmem = pl.BlockSpec(memory_space=pltpu.SMEM), pl.BlockSpec(memory_space=pltpu.VMEM)
    hbm = pl.BlockSpec(memory_space=pl.ANY)
    asked = needed.reshape(1, N_ENT)
    return pl.pallas_call(
        sweep_kernel,
        out_shape=[jax.ShapeDtypeStruct((SLAB, R), BF16), jax.ShapeDtypeStruct((REL_DEV, R, R), F32)],
        in_specs=[vmem] * 4 + [smem] + [hbm] * 4 + [vmem],
        out_specs=[vmem, vmem],
        scratch_shapes=[
            pltpu.VMEM((TILES, BLK, BLK), BF16),
            pltpu.VMEM((N_REL, PIECE, R), BF16),
            pltpu.VMEM((REL_DEV, R, R), BF16),
            pltpu.VMEM((R, R), F32),
            pltpu.VMEM((8, 128), jnp.int32),
            pltpu.VMEM((8, 128), jnp.int32),
            pltpu.VMEM((8, 128), F32),
            pltpu.SMEM((8, 128), jnp.int32),
            pltpu.SMEM((8, 128), F32),
            pltpu.VMEM((N_ENT, N_REL, PIECE, R), BF16),
            pltpu.VMEM((N_ENT, N_REL, PIECE, R), BF16),
            pltpu.VMEM((TILES + 1, BLK, R), F32),
            pltpu.VMEM((N_REL, PIECE, R), F32),
            pltpu.VMEM((N_ENT, BLK, R), BF16),
            pltpu.VMEM((N_ENT, BLK, R), BF16),
            pltpu.VMEM((N_ENT, 8, 128), jnp.int32),
            pltpu.VMEM((N_ENT, 8, 128), jnp.int32),
            pltpu.VMEM((N_ENT, 8, R), F32),
            pltpu.VMEM((N_ENT, 8, R), F32),
            pltpu.VMEM((8, R), F32),
            pltpu.VMEM((N_REL, 8, R), F32),
            pltpu.VMEM((N_ENT, 8, R), F32),
            pltpu.VMEM((128, 128), F32),
            pltpu.VMEM((128, 128), F32),
            pltpu.VMEM((R, R), F32),
            pltpu.VMEM((N_REL, PIECE, R), BF16),
            pltpu.VMEM((N_REL, PIECE, R), BF16),
            pltpu.VMEM((R, R), F32),
            pltpu.VMEM((N_ENT, 16, R), BF16),
            pltpu.VMEM((N_ENT, 16, R), BF16),
            pltpu.VMEM((N_ENT, 16, R), BF16),
            pltpu.SemaphoreType.DMA((2,)),
            pltpu.SemaphoreType.DMA((2, 2, N_ENT)),
            pltpu.SemaphoreType.DMA((9,)),
            pltpu.SemaphoreType.DMA((9,)),
            pltpu.SemaphoreType.DMA((6,)),
        ],
        compiler_params=pltpu.CompilerParams(collective_id=0, has_side_effects=True, vmem_limit_bytes=58 << 20),
        name="sweep",
    )(
        tile_row[0],
        tile_rel[0],
        tile_src[0],
        asked,
        asked,
        tile_vals[0, 0],
        factors.reshape(N_REL, PIECE, R),
        cores,
        basis,
        spectrum.reshape(1, R),
    )


def solution(mesh):
    in_specs = (
        P("ent", "rel", None, None, None),
        P("ent", "rel", None),
        P("ent", "rel", None),
        P("ent", "rel", None),
        P("ent", "rel", None, None),
        P("ent", None),
        P("rel", None, None),
        P(),
        P(),
    )
    out_specs = (P("ent", None), P("rel", None, None))
    return jax.shard_map(
        lambda *args: tuple(shards(*args)), mesh=mesh, in_specs=in_specs, out_specs=out_specs, check_vma=False
    )
```

time: 168 us -> 153 us (0.911)
  Pallas kernels: 157 us -> 148 us
  other arithmetic: 4.65 us -> 0 us
  local copies, waits for them, and re-layouts: 5.68 us -> 3.54 us
    pallas_call x1 -> x0, Pallas kernels: 70.3 us -> none  [shards(): pl.pallas_call(core_kernel, out_shape=[jax.ShapeDtypeStruct((SLAB, R), BF...]
    pallas_call x1, Pallas kernels: 86.6 us -> 148 us  [shards(): pl.pallas_call(sweep_kernel, out_shape=[jax.ShapeDtypeStruct((SLAB, R), B...]
    reduce_sum x4 -> x0, other arithmetic: 2.83 us -> none  [the longest x2 1.09 us: arranged(): rank = jnp.sum(before.astype(jnp.int32), axis=1)]
    unnamed x16 -> x2, local copies, waits for them, and re-layouts: 5.65 us -> 3.54 us
where the time goes in v2:
time: 153 us
  Pallas kernels  148 us (97%)
  local copies, waits for them, and re-layouts  3.54 us (2%)
    pallas_call x1, Pallas kernels, shards(): pl.pallas_call(sweep_kernel, out_shape=[jax.ShapeDtypeStruct((SLAB, R), B...  148 us
    unnamed x2, local copies, waits for them, and re-layouts  3.54 us

profile of v2, /device:TPU:1, one launch (start us, length us, event | category | flops | bytes accessed | tf_op | source)
XLA Modules:
  0.0 152.6 jit_solution(7306310406835929298)
XLA Ops:
  0.6 148.4 %sweep.1 = (bf16[512,256]{1,0:T(8,128)(2,1)}, f32[2,256,256]{2,1,0:T(8,128)}) custom-call(s32[1,64]{1,0:T(1,128)} %bitcast.12, s32[1,64]{1,0:T(1,128)} %bitcast.13, s32[1,64]{1,0:T(1,128)} %bitcast.14, s32[1,32]{1,0:T(1,128)} %bitcast.9, s32[1,32]{1,0:T(1,128)} %bitcast.10, bf16[64,128,128]{2,1,0:T(8,128)(2,1)} %bitcast.7, bf16[8,64,256]{2,1,0:T(8,128)(2,1)} %bitcast.8, ...), custom_call_target="tpu_custom_call" | custom-call | tf_op jit(solution)/shard_map/sweep/pallas_call | solution.py:427
  149.1 1.7 %copy.13 = bf16[512,256]{1,0:T(8,128)(2,1)} copy(bf16[512,256]{1,0:T(8,128)(2,1)} %get-tuple-element.4) | data formatting | bytes 524288
  150.7 1.9 %copy.14 = f32[2,256,256]{2,1,0:T(8,128)} copy(f32[2,256,256]{2,1,0:T(8,128)} %get-tuple-element.5) | data formatting | bytes 1048576

commit v3 on v2

--- a/solution.py
+++ b/solution.py
@@ -143,25 +143,42 @@
     return steps + [finish]
 
 
-def sweep(ref):
+def sweep(ref, spread_column):
     size = ref.shape[0]
     rows = lax.broadcasted_iota(jnp.int32, (size, size), 0)
     lanes = lax.broadcasted_iota(jnp.int32, (size, size), 1)
     lane1 = lax.broadcasted_iota(jnp.int32, (1, size), 1)
-    row1 = lax.broadcasted_iota(jnp.int32, (size, 1), 0)
-
-    def pivot(k, carry):
+
+    def column_of(whole, k):
+        return jnp.broadcast_to(jnp.sum(jnp.where(lanes == k, whole, 0.0), axis=1, keepdims=True), (size, size))
+
+    def pivot(k, column, line):
         whole = ref[...]
-        line = ref[pl.ds(k, 1), :]
-        on_lane = lanes == k
-        column = jnp.sum(jnp.where(on_lane, whole, 0.0), axis=1, keepdims=True)
-        corner = jnp.sum(jnp.where(lane1 == k, line, 0.0), axis=1, keepdims=True)
-        line = jnp.where(lane1 == k, -1.0, line) * (1.0 / corner)
-        column = jnp.where(row1 == k, -1.0, column)
-        ref[...] = jnp.where(on_lane | (rows == k), 0.0, whole) - column * line
-        return carry
-
-    return pivot
+        later = jnp.minimum(k + 1, size - 1)
+        next_column = column_of(whole, k + 1)
+        next_line = ref[pl.ds(later, 1), :]
+        spread_column[...] = column
+        scale = 1.0 / spread_column[pl.ds(k, 1), :]
+        factor = spread_column[pl.ds(later, 1), :]
+        line = jnp.where(lane1 == k, -1.0, line) * scale
+        column = jnp.where(rows == k, -1.0, column)
+        ref[...] = jnp.where((lanes == k) | (rows == k), 0.0, whole) - column * line
+        next_column = jnp.where(rows == k, 0.0, next_column) - column * (factor * scale)
+        next_line = jnp.where(lane1 == k, 0.0, next_line) - factor * line
+        return next_column, next_line
+
+    def start():
+        return column_of(ref[...], 0), ref[0:1, :]
+
+    def some(k, count, carry):
+        def four(q, carry):
+            for i in range(4):
+                carry = pivot(k + q * 4 + i, *carry)
+            return carry
+
+        return lax.fori_loop(0, count // 4, four, carry)
+
+    return start, some
 
 
 def sorted_sums(run, count, term, keep_at, start):
@@ -198,7 +215,7 @@
     factors_out, cores_out,
     tiles, factors, cores, basis, raw, meta_wide, keeps_wide, meta, keeps,
     table, fresh, run, ahead_terms, terms, landed, req_out, req_in, sys_out, sys_in, sys_row, sys_rows, sys_all,
-    corner, band, inverse, numer_out, numer_in, weight, sum_out, sum_in, sum_all,
+    corner, spread_column, band, inverse, numer_out, numer_in, weight, sum_out, sum_in, sum_all,
     ring_send, ring_recv, pair_send, pair_recv, local,
 ):
     ent = lax.axis_index("ent")
@@ -286,47 +303,55 @@
     def backward_part(q):
         sorted_sums(run, 16, backward, lambda t: keeps[1, t], q * 16)
 
+    def pack(o):
+        return (run[meta[7, o]] * keeps[3, o]).astype(BF16)
+
+    def give(k, carry):
+        o = lax.rem(ent + k, N_ENT)
+        terms[o] = pack(o)
+        send(terms.at[o], landed.at[ent], pair_send.at[5], pair_recv.at[5], {"ent": o}).start()
+        return carry
+
     backward_part(0)
+    backward_part(1)
     spread_wait(N_ENT, sys_in, sys_out, pair_send.at[0], pair_recv.at[0])
     sys_row[...] = jnp.sum(sys_in[...], axis=0)
     spread("rel", N_REL, rel, lambda o: sys_row, sys_rows, pair_send.at[3], pair_recv.at[3])
     sys_rows[rel] = sys_row[...]
     steps.pop(0)()
-    backward_part(1)
+    backward_part(2)
     steps.pop(0)()
-    backward_part(2)
+    backward_part(3)
     spread_wait(N_REL, sys_rows, sys_row, pair_send.at[3], pair_recv.at[3])
     unit = lax.broadcasted_iota(jnp.int32, (8, R), 0) + ent * 8 == lax.broadcasted_iota(jnp.int32, (8, R), 1)
     sys_all[ent] = jnp.sum(sys_rows[...], axis=0) + jnp.where(unit, ridge_shift, 0.0)
     spread("ent", N_ENT, ent, lambda o: sys_all.at[ent], sys_all, pair_send.at[4], pair_recv.at[4])
     steps.pop(0)()
-    backward_part(3)
-    steps.pop(0)()
-
-    def pack(o):
-        return (run[meta[7, o]] * keeps[3, o]).astype(BF16)
-
-    def give(k, carry):
-        o = lax.rem(ent + k, N_ENT)
-        terms[o] = pack(o)
-        send(terms.at[o], landed.at[ent], pair_send.at[5], pair_recv.at[5], {"ent": o}).start()
-        return carry
-
-    lax.fori_loop(1, N_ENT, give, 0)
     landed[ent] = pack(ent)
-    steps.pop(0)()
+    given = [1]
+
+    def advance(count):
+        if len(steps) > 1:
+            steps.pop(0)()
+            count = N_ENT if len(steps) == 1 else count
+        upto = min(N_ENT, given[0] + count)
+        lax.fori_loop(given[0], upto, give, 0)
+        given[0] = upto
+
+    for _ in range(3):
+        advance(1)
     spread_wait(N_ENT, sys_all, sys_all, pair_send.at[4], pair_recv.at[4])
 
     system = sys_all[...].reshape(R, R)
     corner[...] = system[:128, :128]
     band[...] = system[:128, 128:]
-    pivot = sweep(corner)
+    start, some_pivots = sweep(corner, spread_column)
 
     def pivots():
+        carry = start()
         for i in range(8):
-            if len(steps) > 1:
-                steps.pop(0)()
-            lax.fori_loop(i * 16, i * 16 + 16, pivot, 0)
+            advance(1)
+            carry = some_pivots(i * 16, 16, carry)
 
     pivots()
     first = -corner[...]
@@ -454,6 +479,7 @@
             pltpu.VMEM((N_ENT, 8, R), F32),
             pltpu.VMEM((128, 128), F32),
             pltpu.VMEM((128, 128), F32),
+            pltpu.VMEM((128, 128), F32),
             pltpu.VMEM((R, R), F32),
             pltpu.VMEM((N_REL, PIECE, R), BF16),
             pltpu.VMEM((N_REL, PIECE, R), BF16),

time: 153 us -> 140 us (0.915)
  Pallas kernels: 148 us -> 136 us
    pallas_call x1, Pallas kernels: 148 us -> 136 us  [shards(): pl.pallas_call(sweep_kernel, out_shape=[jax.ShapeDtypeStruct((SLAB, R), B...]
where the time goes in v3:
time: 140 us
  Pallas kernels  136 us (97%)
  local copies, waits for them, and re-layouts  3.54 us (3%)
    pallas_call x1, Pallas kernels, shards(): pl.pallas_call(sweep_kernel, out_shape=[jax.ShapeDtypeStruct((SLAB, R), B...  136 us
    unnamed x2, local copies, waits for them, and re-layouts  3.54 us

profile of v3, /device:TPU:1, one launch (start us, length us, event | category | flops | bytes accessed | tf_op | source)
XLA Modules:
  0.0 139.8 jit_solution(15161849828058440130)
XLA Ops:
  0.6 135.6 %sweep.1 = (bf16[512,256]{1,0:T(8,128)(2,1)}, f32[2,256,256]{2,1,0:T(8,128)}) custom-call(s32[1,64]{1,0:T(1,128)} %bitcast.12, s32[1,64]{1,0:T(1,128)} %bitcast.13, s32[1,64]{1,0:T(1,128)} %bitcast.14, s32[1,32]{1,0:T(1,128)} %bitcast.9, s32[1,32]{1,0:T(1,128)} %bitcast.10, bf16[64,128,128]{2,1,0:T(8,128)(2,1)} %bitcast.7, bf16[8,64,256]{2,1,0:T(8,128)(2,1)} %bitcast.8, ...), custom_call_target="tpu_custom_call" | custom-call | tf_op jit(solution)/shard_map/sweep/pallas_call | solution.py:452
  136.3 1.7 %copy.13 = bf16[512,256]{1,0:T(8,128)(2,1)} copy(bf16[512,256]{1,0:T(8,128)(2,1)} %get-tuple-element.4) | data formatting | bytes 524288
  138.0 1.9 %copy.14 = f32[2,256,256]{2,1,0:T(8,128)} copy(f32[2,256,256]{2,1,0:T(8,128)} %get-tuple-element.5) | data formatting | bytes 1048576

commit v4 on v3

--- a/solution.py
+++ b/solution.py
@@ -10,6 +10,7 @@
 N_ENT, N_REL = 32, 8
 BLK, R, ROWS, TILES, REL_DEV, SLAB = 128, 256, 4, 64, 2, 512
 PIECE = SLAB // N_REL
+EARLY = N_ENT // 2
 MESH = pl.DeviceIdType.MESH
 F32, BF16 = jnp.float32, jnp.bfloat16
 HIGH = lax.Precision.HIGHEST
@@ -220,6 +221,7 @@
 ):
     ent = lax.axis_index("ent")
     rel = lax.axis_index("rel")
+    all_here = greet(ent, rel)
     moves = [
         pltpu.make_async_copy(a, b, local.at[i])
         for i, (a, b) in enumerate(
@@ -228,7 +230,6 @@
     ]
     for move in moves:
         move.start()
-    all_here = greet(ent, rel)
 
     moves[0].wait()
     moves[1].wait()
@@ -283,7 +284,7 @@
         order.start()
 
     def ask(o, carry):
-        req_out[o] = jnp.full((8, 128), needed[0, o], jnp.int32)
+        req_out[o] = jnp.full((1, 128), needed[0, o], jnp.int32)
         return carry
 
     lax.fori_loop(0, N_ENT, ask, 0)
@@ -306,11 +307,14 @@
     def pack(o):
         return (run[meta[7, o]] * keeps[3, o]).astype(BF16)
 
-    def give(k, carry):
-        o = lax.rem(ent + k, N_ENT)
-        terms[o] = pack(o)
-        send(terms.at[o], landed.at[ent], pair_send.at[5], pair_recv.at[5], {"ent": o}).start()
-        return carry
+    def giver(group):
+        def give(k, carry):
+            o = lax.rem(ent + k, N_ENT)
+            terms[o] = pack(o)
+            send(terms.at[o], landed.at[ent], pair_send.at[group], pair_recv.at[group], {"ent": o}).start()
+            return carry
+
+        return give
 
     backward_part(0)
     backward_part(1)
@@ -335,11 +339,13 @@
             steps.pop(0)()
             count = N_ENT if len(steps) == 1 else count
         upto = min(N_ENT, given[0] + count)
-        lax.fori_loop(given[0], upto, give, 0)
+        middle = min(max(given[0], EARLY), upto)
+        lax.fori_loop(given[0], middle, giver(5), 0)
+        lax.fori_loop(middle, upto, giver(9), 0)
         given[0] = upto
 
     for _ in range(3):
-        advance(1)
+        advance(2)
     spread_wait(N_ENT, sys_all, sys_all, pair_send.at[4], pair_recv.at[4])
 
     system = sys_all[...].reshape(R, R)
@@ -350,7 +356,7 @@
     def pivots():
         carry = start()
         for i in range(8):
-            advance(1)
+            advance(2)
             carry = some_pivots(i * 16, 16, carry)
 
     pivots()
@@ -387,26 +393,35 @@
     wide = jnp.broadcast_to(spectrum[...], (R, R))
     weight[...] = 1.0 / (wide * wide.T + ridge_shift)
     spread_wait(N_ENT, req_in, req_out, pair_send.at[1], pair_recv.at[1])
-    spread_wait(N_ENT, landed, terms, pair_send.at[5], pair_recv.at[5])
-
-    def landing(q):
+    spread_wait(EARLY, landed, terms, pair_send.at[5], pair_recv.at[5])
+
+    def landing(q, least, most, total):
         block = q // 2
         chunk = pl.ds(pl.multiple_of(lax.rem(q, 2) * PIECE, PIECE), PIECE)
 
-        def add(o, total):
-            return total + jnp.where(jnp.tile(req_in[o], (8, 2)) == block, landed[o, chunk, :].astype(F32), 0.0)
-
-        return lax.fori_loop(0, N_ENT, add, ahead_terms[q])
+        def add(k, total):
+            o = lax.rem(ent - k + N_ENT, N_ENT)
+            asked = jnp.broadcast_to(jnp.concatenate([req_in[o]] * 2, axis=1), (PIECE, R))
+            return total + jnp.where(asked == block, landed[o, chunk, :].astype(F32), 0.0)
+
+        return lax.fori_loop(least, most, add, total)
+
+    def early(q, carry):
+        ahead_terms[q] = landing(q, 0, EARLY, ahead_terms[q])
+        return carry
+
+    lax.fori_loop(0, N_REL, early, 0)
+    spread_wait(N_ENT - EARLY + 1, landed, terms, pair_send.at[9], pair_recv.at[9])
 
     def hand_over(k, carry):
         z = lax.rem(rel + k, N_REL)
-        numer_out[z] = landing(z).astype(BF16)
+        numer_out[z] = landing(z, EARLY, N_ENT, ahead_terms[z]).astype(BF16)
         send(numer_out.at[z], numer_in.at[rel], pair_send.at[2], pair_recv.at[2], {"rel": z}).start()
         return carry
 
     lax.fori_loop(1, N_REL, hand_over, 0)
     numer_in[rel] = jnp.zeros((PIECE, R), BF16)
-    mine = landing(rel)
+    mine = landing(rel, EARLY, N_ENT, ahead_terms[rel])
     spread_wait(N_REL, numer_in, numer_out, pair_send.at[2], pair_recv.at[2])
     total = mine + jnp.sum(numer_in[...].astype(F32), axis=0)
     fresh[ent, rel] = dot(total, inverse[...], precision=HIGH).astype(BF16)
@@ -470,8 +485,8 @@
             pltpu.VMEM((N_REL, PIECE, R), F32),
             pltpu.VMEM((N_ENT, BLK, R), BF16),
             pltpu.VMEM((N_ENT, BLK, R), BF16),
-            pltpu.VMEM((N_ENT, 8, 128), jnp.int32),
-            pltpu.VMEM((N_ENT, 8, 128), jnp.int32),
+            pltpu.VMEM((N_ENT, 1, 128), jnp.int32),
+            pltpu.VMEM((N_ENT, 1, 128), jnp.int32),
             pltpu.VMEM((N_ENT, 8, R), F32),
             pltpu.VMEM((N_ENT, 8, R), F32),
             pltpu.VMEM((8, R), F32),
@@ -489,8 +504,8 @@
             pltpu.VMEM((N_ENT, 16, R), BF16),
             pltpu.SemaphoreType.DMA((2,)),
             pltpu.SemaphoreType.DMA((2, 2, N_ENT)),
-            pltpu.SemaphoreType.DMA((9,)),
-            pltpu.SemaphoreType.DMA((9,)),
+            pltpu.SemaphoreType.DMA((10,)),
+            pltpu.SemaphoreType.DMA((10,)),
             pltpu.SemaphoreType.DMA((6,)),
         ],
         compiler_params=pltpu.CompilerParams(collective_id=0, has_side_effects=True, vmem_limit_bytes=58 << 20),

time: 140 us -> 138 us (0.986)
  Pallas kernels: 136 us -> 134 us
    pallas_call x1, Pallas kernels: 136 us -> 134 us  [shards(): pl.pallas_call(sweep_kernel, out_shape=[jax.ShapeDtypeStruct((SLAB, R), B...]
where the time goes in v4:
time: 138 us
  Pallas kernels  134 us (97%)
  local copies, waits for them, and re-layouts  3.54 us (3%)
    pallas_call x1, Pallas kernels, shards(): pl.pallas_call(sweep_kernel, out_shape=[jax.ShapeDtypeStruct((SLAB, R), B...  134 us
    unnamed x2, local copies, waits for them, and re-layouts  3.54 us

profile of v4, /device:TPU:1, one launch (start us, length us, event | category | flops | bytes accessed | tf_op | source)
XLA Modules:
  0.0 137.8 jit_solution(13807328407753509039)
XLA Ops:
  0.6 133.6 %sweep.1 = (bf16[512,256]{1,0:T(8,128)(2,1)}, f32[2,256,256]{2,1,0:T(8,128)}) custom-call(s32[1,64]{1,0:T(1,128)} %bitcast.12, s32[1,64]{1,0:T(1,128)} %bitcast.13, s32[1,64]{1,0:T(1,128)} %bitcast.14, s32[1,32]{1,0:T(1,128)} %bitcast.9, s32[1,32]{1,0:T(1,128)} %bitcast.10, bf16[64,128,128]{2,1,0:T(8,128)(2,1)} %bitcast.7, bf16[8,64,256]{2,1,0:T(8,128)(2,1)} %bitcast.8, ...), custom_call_target="tpu_custom_call" | custom-call | tf_op jit(solution)/shard_map/sweep/pallas_call | solution.py:467
  134.2 1.7 %copy.13 = bf16[512,256]{1,0:T(8,128)(2,1)} copy(bf16[512,256]{1,0:T(8,128)(2,1)} %get-tuple-element.4) | data formatting | bytes 524288
  135.9 1.9 %copy.14 = f32[2,256,256]{2,1,0:T(8,128)} copy(f32[2,256,256]{2,1,0:T(8,128)} %get-tuple-element.5) | data formatting | bytes 1048576

commit v5 on v4

--- a/solution.py
+++ b/solution.py
@@ -183,13 +183,13 @@
 
 
 def sorted_sums(run, count, term, keep_at, start):
-    def four(q, carry):
-        for i in range(4):
-            t = start + q * 4 + i
+    def eight(q, carry):
+        for i in range(8):
+            t = start + q * 8 + i
             run[t + 1] = run[t] * keep_at(t) + term(t)
         return carry
 
-    lax.fori_loop(0, count // 4, four, 0)
+    lax.fori_loop(0, count // 8, eight, 0)
 
 
 def arranged(raw, key):

time: 138 us -> 137 us (level)
  no operation moved by 1% of the time
where the time goes in v5:
time: 137 us
  Pallas kernels  133 us (97%)
  local copies, waits for them, and re-layouts  3.54 us (3%)
    pallas_call x1, Pallas kernels, shards(): pl.pallas_call(sweep_kernel, out_shape=[jax.ShapeDtypeStruct((SLAB, R), B...  133 us
    unnamed x2, local copies, waits for them, and re-layouts  3.54 us

profile of v5, /device:TPU:1, one launch (start us, length us, event | category | flops | bytes accessed | tf_op | source)
XLA Modules:
  0.0 137.0 jit_solution(6982081971547256701)
XLA Ops:
  0.6 132.8 %sweep.1 = (bf16[512,256]{1,0:T(8,128)(2,1)}, f32[2,256,256]{2,1,0:T(8,128)}) custom-call(s32[1,64]{1,0:T(1,128)} %bitcast.12, s32[1,64]{1,0:T(1,128)} %bitcast.13, s32[1,64]{1,0:T(1,128)} %bitcast.14, s32[1,32]{1,0:T(1,128)} %bitcast.9, s32[1,32]{1,0:T(1,128)} %bitcast.10, bf16[64,128,128]{2,1,0:T(8,128)(2,1)} %bitcast.7, bf16[8,64,256]{2,1,0:T(8,128)(2,1)} %bitcast.8, ...), custom_call_target="tpu_custom_call" | custom-call | tf_op jit(solution)/shard_map/sweep/pallas_call | solution.py:467
  133.4 1.7 %copy.13 = bf16[512,256]{1,0:T(8,128)(2,1)} copy(bf16[512,256]{1,0:T(8,128)(2,1)} %get-tuple-element.4) | data formatting | bytes 524288
  135.1 1.9 %copy.14 = f32[2,256,256]{2,1,0:T(8,128)} copy(f32[2,256,256]{2,1,0:T(8,128)} %get-tuple-element.5) | data formatting | bytes 1048576
